TPU v7x, 256 devices: a whole 4x4x8 slice. The times are simulated.
256 devices in a mesh: mat: 2 (over y_lo), band: 8 (over x, core), col: 16 (over z, y_hi).
Axes of the slice: x: 4, y: 4 (y_hi: 2, y_lo: 2; y = y_hi * 2 + y_lo), z: 8, core: 2. Of those that a mesh axis runs over, the one named last changes fastest.
Arguments:
- iterate: float32 [8192, 18432], P(('mat', 'band'), 'col'), parts along dimension 0, may hold values from -6 to 6
Outputs:
- next_iterate: float32 [8192, 18432], P(('mat', 'band'), 'col'), parts along dimension 0
There are 2 independent parts, one for each index of `mat`. A program takes and returns all parts, laid end to end along the dimension named above; each array names one. Nothing has to cross between parts.
All inputs are finite; a program needn't handle non-finite values.
Results may differ from a plain program's by a relative error of at most 0.012.
The roundings to bfloat16 on the way count: a program that leaves them out, or rounds other values in their place, can miss the bound.
Values may be sent and summed in bfloat16 or wider, within the bound.
A program may use at most 128 MiB of HBM per device.

v0:
```python
import jax
import jax.numpy as jnp
from jax import lax
from jax.sharding import PartitionSpec as P

COLS = 18432


linear_coef = 3.4445
cubic_coef = -4.775
quintic_coef = 2.0315


def shards(iterate):
    narrow = iterate.astype(jnp.bfloat16)
    rows_all = lax.all_gather(narrow, "band", axis=0, tiled=True)
    chosen = rows_all
    gram_tile = (
        lax.psum_scatter(
            lax.dot_general(
                chosen, narrow, (((1,), (1,)), ((), ())), preferred_element_type=jnp.float32
            ),
            "col",
            scatter_dimension=0,
            tiled=True,
        )
        / COLS
    )
    gram_band = lax.all_gather(gram_tile.astype(jnp.bfloat16), "col", axis=0, tiled=True)
    chosen = gram_band
    square_tile = jnp.dot(
        lax.all_gather(gram_tile.astype(jnp.bfloat16), "band", axis=1, tiled=True),
        chosen,
        preferred_element_type=jnp.float32,
    )
    poly_tile = (cubic_coef * gram_tile + quintic_coef * square_tile).astype(jnp.bfloat16)
    chosen = rows_all
    applied = lax.dot_general(
        lax.all_gather(poly_tile, "col", axis=0, tiled=True),
        chosen,
        (((0,), (0,)), ((), ())),
        preferred_element_type=jnp.float32,
    )
    return linear_coef * iterate + applied


def solution(mesh):
    return jax.shard_map(
        shards,
        mesh=mesh,
        in_specs=(P(("mat", "band"), "col"),),
        out_specs=P(("mat", "band"), "col"),
        check_vma=False,
    )
```

profile of v0, /device:TPU:1, one launch (start us, length us, event | category | flops | bytes accessed | tf_op | source)
XLA Modules:
  0.0 552.3 jit_solution(6499395635037874434)
XLA Ops:
  6.5 0.0 all-gather.5.cloned.1.call-start
  6.5 2.8 convert_element_type.10
  9.3 0.0 all-gather.5.cloned.1.call-update
  9.4 0.0 reduce-scatter.2.cloned.1.call-start
  9.4 61.0 %all-gather.5.cloned.1.call-done = bf16[4096,1152]{1,0:T(8,128)(2,1)} async-done(((bf16[512,1152]{1,0:T(8,128)(2,1)}), bf16[4096,1152]{1,0:T(8,128)(2,1)}) %all-gather.5.cloned.1.call-update) | async-done | bytes 9437200 | tf_op jit(solution)/shard_map/all_gather | solution.py:16
  70.4 11.8 %fusion.2 = f32[4096,512]{1,0:T(8,128)} fusion(bf16[4096,1152]{1,0:T(8,128)(2,1)} %all-gather.5.cloned.1.call-done, bf16[512,1152]{1,0:T(8,128)(2,1)} %convert_element_type.10), kind=kOutput, calls=%fused_computation.5 | convolution fusion | flops 4831838208 | bytes 19005440 | tf_op jit(solution)/shard_map/dot_general | solution.py:20
  82.1 0.0 reduce-scatter.2.cloned.1.call-update
  82.2 0.0 all-gather.7.cloned.1.call-start
  82.2 218.9 %reduce-scatter.2.cloned.1.call-done = f32[256,512]{1,0:T(8,128)} async-done(((f32[4096,512]{1,0:T(8,128)}), f32[256,512]{1,0:T(8,128)}) %reduce-scatter.2.cloned.1.call-update) | async-done | bytes 524304 | tf_op jit(solution)/shard_map/reduce_scatter | solution.py:19
  301.1 1.8 multiply_convert_fusion
  302.9 0.0 all-gather.7.cloned.1.call-update
  302.9 0.0 copy-start
  303.0 0.0 all-gather.9.cloned.1.call-start
  303.0 0.5 all-gather.9.cloned.1.call-update
  303.5 0.0 all-gather.11.cloned.1.call-start
  303.6 30.3 %all-gather.7.cloned.1.call-done = bf16[256,4096]{1,0:T(8,128)(2,1)} async-done(((bf16[256,512]{1,0:T(8,128)(2,1)}), bf16[256,4096]{1,0:T(8,128)(2,1)}) %all-gather.7.cloned.1.call-update) | async-done | bytes 2097168 | tf_op jit(solution)/shard_map/all_gather | solution.py:32
  333.9 99.2 %all-gather.9.cloned.1.call-done = bf16[4096,512]{1,0:T(8,128)(2,1)} async-done(((bf16[256,512]{1,0:T(8,128)(2,1)}), bf16[4096,512]{1,0:T(8,128)(2,1)}) %all-gather.9.cloned.1.call-update) | async-done | bytes 4194320 | tf_op jit(solution)/shard_map/all_gather | solution.py:29
  433.1 4.9 fusion.1
  437.9 0.0 all-gather.11.cloned.1.call-update
  437.9 96.7 %all-gather.11.cloned.1.call-done = bf16[4096,512]{1,0:T(8,128)(2,1)} async-done(((bf16[256,512]{1,0:T(8,128)(2,1)}), bf16[4096,512]{1,0:T(8,128)(2,1)}) %all-gather.11.cloned.1.call-update) | async-done | bytes 4194320 | tf_op jit(solution)/shard_map/all_gather | solution.py:39
  534.6 0.0 copy-done
  534.6 11.2 %convolution_add_fusion = f32[512,1152]{1,0:T(8,128)} fusion(bf16[4096,512]{1,0:T(8,128)(2,1)} %all-gather.11.cloned.1.call-done, bf16[4096,1152]{1,0:T(8,128)(2,1)} %all-gather.5.cloned.1.call-done, f32[512,1152]{1,0:T(8,128)S(1)} %copy-done), kind=kOutput, calls=%fused_computation | convolution fusion | flops 4833017856 | bytes 18350080 | tf_op jit(solution)/shard_map/dot_general | solution.py:38
Async XLA Ops:
  6.5 63.9 %all-gather.5.cloned.1.call-start = ((), (), s32[]{:S(2)}) async-start(), calls=%async_computation.1 | async-start | bytes 10616832 | tf_op jit(solution)/shard_map/all_gather | solution.py:16
  9.4 291.8 %reduce-scatter.2.cloned.1.call-start = ((), (), s32[]{:S(2)}) async-start(), calls=%async_computation.2 | async-start | bytes 8912896 | tf_op jit(solution)/shard_map/reduce_scatter | solution.py:19
  82.2 251.7 %all-gather.7.cloned.1.call-start = ((), (), s32[]{:S(2)}) async-start(), calls=%async_computation.3 | async-start | bytes 2359296 | tf_op jit(solution)/shard_map/all_gather | solution.py:32
  302.9 231.7 %copy-start = (f32[512,1152]{1,0:T(8,128)S(1)}, f32[512,1152]{1,0:T(8,128)}, u32[]{:S(2)}) copy-start(f32[512,1152]{1,0:T(8,128)} %param.1) | copy-start | bytes 7077892
  303.0 130.1 %all-gather.9.cloned.1.call-start = ((), (), s32[]{:S(2)}) async-start(), calls=%async_computation.4 | async-start | bytes 4456448 | tf_op jit(solution)/shard_map/all_gather | solution.py:29
  303.5 231.1 %all-gather.11.cloned.1.call-start = ((), (), s32[]{:S(2)}) async-start(), calls=%async_computation.5 | async-start | bytes 4456448 | tf_op jit(solution)/shard_map/all_gather | solution.py:39
Sparse Core Ops, SparseCore 0:
  9.5 60.8 all-gather.4
  82.3 218.7 reduce-scatter.1
  303.1 30.7 all-gather.6
  336.3 96.6 all-gather.8
  438.1 96.5 all-gather.10
where the time goes:
time: 555 us; the launch traced here: 552 us
  waiting for transfers between devices  507 us (91%)
  matrix products  27.8 us (5%)
  between operations  13.1 us (2%)
    reduce_scatter x1, waiting for transfers between devices, shards(): lax.psum_scatter(lax.dot_general(chosen, narrow, (((1,), (1,)), ((), ()))...  219 us
    all_gather x1, waiting for transfers between devices, shards(): lax.all_gather(gram_tile.astype(jnp.bfloat16), 'col', axis=0, tiled=True)  99.2 us
    all_gather x1, waiting for transfers between devices, shards(): lax.all_gather(poly_tile, 'col', axis=0, tiled=True)  96.7 us
    all_gather x1, waiting for transfers between devices, shards(): rows_all = lax.all_gather(narrow, 'band', axis=0, tiled=True)  61 us
    all_gather x1, waiting for transfers between devices, shards(): lax.all_gather(gram_tile.astype(jnp.bfloat16), 'band', axis=1, tiled=True)  30.3 us
    dot_general x1, matrix products, shards(): lax.dot_general(chosen, narrow, (((1,), (1,)), ((), ())), preferred_eleme...  11.8 us
    dot_general x1, matrix products, shards(): lax.dot_general(lax.all_gather(poly_tile, 'col', axis=0, tiled=True), cho...  11.2 us
  transfers between devices with their start and end apart: 5, of which 5 were waited for; matrix products, arithmetic and copies ran while one was open for 0% of the time, Pallas kernels for 0%

commit v1 on v0

v1 whole, which is shorter than its diff:
```python
import jax
import jax.numpy as jnp
from jax import lax
from jax.experimental import pallas as pl
from jax.experimental.pallas import tpu as pltpu
from jax.sharding import PartitionSpec as P

COLS = 18432
MESH = pl.DeviceIdType.MESH
linear_coef = 3.4445
cubic_coef = -4.775
quintic_coef = 2.0315

F32, BF16 = jnp.float32, jnp.bfloat16
BLOCK, WIDTH, TICKS, UNIT = 512, 1152, 8, 64
ROWS = BLOCK * TICKS
SPLIT = 1536
MESSAGES = 400
START = (0, 1, 3, 5, 7, 9, 10, 11)


def dot(a, b, contract):
    return lax.dot_general(a, b, (((1,), (contract,)), ((), ())), preferred_element_type=F32)


def kernel(x_ref, o_ref, X, N, Y, V, G, SB0, RB0, SB, RB, YS, YR, FS, FR, GS, DS, DR, DB, YA, ssem, rsem, lsem):
    mat, band, col = lax.axis_index("mat"), lax.axis_index("band"), lax.axis_index("col")
    x, core = lax.div(band, 2), lax.rem(band, 2)
    z, y = lax.div(col, 2), lax.rem(col, 2)
    other = 1 - y

    def at_x(d):
        return (mat, lax.rem(x + d + 4, 4) * 2 + core, col)

    def zi(d):
        return lax.rem(z + d + 8, 8)

    def at_z(d):
        return (mat, band, zi(d) * 2 + y)

    XP, XM, ZP, ZM = at_x(1), at_x(-1), at_z(1), at_z(-1)
    YP = (mat, band, z * 2 + other)
    CP = (mat, x * 2 + 1 - core, col)

    started = []

    def send(src, dst, peer):
        n = len(started)
        copy = pltpu.make_async_remote_copy(
            src_ref=src, dst_ref=dst, send_sem=ssem.at[n], recv_sem=rsem.at[n], device_id=peer, device_id_type=MESH
        )
        copy.start()
        started.append(copy)
        return copy

    loads = [pltpu.make_async_copy(x_ref.at[pl.ds(UNIT * u, UNIT)], X.at[u], lsem.at[u]) for u in range(8)]
    for load in loads:
        load.start()
    barrier = pltpu.get_barrier_semaphore()
    for peer in (XP, XM, ZP, ZM, YP, CP):
        pl.semaphore_signal(barrier, inc=1, device_id=peer, device_id_type=MESH)
    for u, load in enumerate(loads):
        load.wait()
        N[0, u] = X[u].astype(BF16)
    pl.semaphore_wait(barrier, 6)

    plus, minus, pair, hop, hop_pair = {}, {}, {}, {}, {}
    relay = {}

    def send_own(i):
        plus[i] = send(N.at[0, pl.ds(2 * i, 2)], N.at[2 + i, pl.ds(0, 2)], XP)
        minus[i] = send(N.at[0, pl.ds(2 * i, 2)], N.at[2 + i, pl.ds(4, 2)], XM)

    def send_hop(i):
        if i < 2:
            hop[i] = send(N.at[2 + i, pl.ds(0, 2)], N.at[6, pl.ds(2 * i, 2)], XP)
        else:
            hop[i] = send(N.at[2 + i, pl.ds(4, 2)], N.at[6, pl.ds(2 * i, 2)], XM)

    def pass_hop(i):
        hop[i].wait_recv()
        hop_pair[i] = send(N.at[6, pl.ds(2 * i, 2)], N.at[7, pl.ds(2 * i, 2)], CP)

    send_own(0)
    pair_block = send(N.at[0], N.at[1], CP)
    send_own(1)

    def arrive(t):
        if t == 1:
            pair_block.wait_recv()
        if 2 <= t <= 5:
            i = t - 2
            plus[i].wait_recv()
            relay[i, 0] = send(N.at[t, pl.ds(0, 2)], N.at[t, pl.ds(2, 2)], CP)
            minus[i].wait_recv()
            relay[i, 1] = send(N.at[t, pl.ds(4, 2)], N.at[t, pl.ds(6, 2)], CP)
            if i < 2:
                send_own(i + 2)
            else:
                send_hop(i - 2)
                send_hop(i)
            relay[i, 0].wait_recv()
            relay[i, 1].wait_recv()

    first, step0, step, last, moved = {}, {}, {}, {}, {}
    diag = {}

    def gram(t):
        arrive(t)
        if t <= 5:
            right = N[t].reshape(BLOCK, WIDTH)
        elif t == 6:
            right = N[2:6, 4:6].reshape(BLOCK, WIDTH)
        else:
            right = N[2:6, 2:4].reshape(BLOCK, WIDTH)
        total = jnp.zeros((1, BLOCK), F32)
        for m in range(2):
            if t <= 5:
                left = N[0, 4 * m : 4 * m + 4].reshape(256, WIDTH)
            elif t == 6:
                left = N[2 + 2 * m : 4 + 2 * m, 0:2].reshape(256, WIDTH)
            else:
                left = N[2 + 2 * m : 4 + 2 * m, 4:6].reshape(256, WIDTH)
            p = dot(left, right, 1)
            if t == 0:
                rows = lax.broadcasted_iota(jnp.int32, (256, BLOCK), 0) + 256 * m
                lanes = lax.broadcasted_iota(jnp.int32, (256, BLOCK), 1)
                total += jnp.sum(jnp.where(rows == lanes, p, 0.0), axis=0, keepdims=True)
            p = p.reshape(4, UNIT, BLOCK)
            low, high = p[:, 0:32, 256:], p[:, 32:64, 256:]
            V[t, 4 * m : 4 * m + 4, 0:64, :] = p[:, :, 0:256]
            V[t, 4 * m : 4 * m + 4, 64:96, :] = jnp.where(y == 0, low, high)
            YS[t, 4 * m : 4 * m + 4] = jnp.where(y == 0, high, low).astype(BF16)
        first[t] = send(YS.at[t], YR.at[t], YP)
        if t == 0:
            DS[...] = jnp.broadcast_to(total, (8, BLOCK))
            diag["y"] = send(DS, DR, YP)

    def stage1(t):
        first[t].wait_recv()
        V[t, :, 64:96, :] += YR[t].astype(F32)
        d = zi(4)
        SB0[t, 0] = V[t, d, :, 0:128].astype(BF16)
        SB0[t, 1] = V[t, d, :, 128:256].astype(BF16)
        step0[t] = (send(SB0.at[t, 0], RB0.at[t, 0], ZP), send(SB0.at[t, 1], RB0.at[t, 1], ZM))

    def stage2(t):
        step0[t][0].wait_recv()
        d = zi(3)
        SB[t, 0, 0, :, 0:128] = (V[t, d, :, 0:128] + RB0[t, 0].astype(F32)).astype(BF16)
        SB[t, 0, 0, :, 128:256] = V[t, d, :, 128:256].astype(BF16)
        up = send(SB.at[t, 0, 0], RB.at[t, 0, 0], ZP)
        step0[t][1].wait_recv()
        d = zi(-3)
        SB[t, 1, 0, :, 0:128] = V[t, d, :, 0:128].astype(BF16)
        SB[t, 1, 0, :, 128:256] = (V[t, d, :, 128:256] + RB0[t, 1].astype(F32)).astype(BF16)
        step[t, 0] = (up, send(SB.at[t, 1, 0], RB.at[t, 1, 0], ZM))

    def stage34(t, n):
        both = []
        for way, peer in ((0, ZP), (1, ZM)):
            step[t, n - 1][way].wait_recv()
            d = zi(3 - n) if way == 0 else zi(n - 3)
            SB[t, way, n] = (V[t, d] + RB[t, way, n - 1].astype(F32)).astype(BF16)
            both.append(send(SB.at[t, way, n], RB.at[t, way, n], peer))
        step[t, n] = both

    def stage5(t):
        step[t, 2][0].wait_recv()
        step[t, 2][1].wait_recv()
        r = V[t, z] + RB[t, 0, 2].astype(F32) + RB[t, 1, 2].astype(F32)
        V[t, z] = r
        FS[t] = jnp.where(y == 0, r[32:64], r[0:32]).astype(BF16)
        last[t] = send(FS.at[t], FR.at[t], YP)

    def stage6(t):
        last[t].wait_recv()
        r = V[t, z]
        mine = jnp.where(y == 0, r[0:32], r[32:64]) + FR[t].astype(F32)
        g = jnp.concatenate([mine, r[64:96]], axis=1) * (1.0 / COLS)
        if t == 0:
            rows = lax.broadcasted_iota(jnp.int32, (32, BLOCK), 0) + (z * 64 + y * 32)
            lanes = lax.broadcasted_iota(jnp.int32, (32, BLOCK), 1)
            g = jnp.where(rows == lanes, DS[0:1], g)
        g = g.astype(BF16)
        if t <= 5:
            G[z, y, :, BLOCK * t : BLOCK * (t + 1)] = g
        else:
            GS[t - 6] = g
            there = G.at[z, y, :, pl.ds(BLOCK * t, BLOCK)]
            moved[t] = send(GS.at[t - 6], there, XM if t == 6 else XP)

    def diag_step(r):
        if r == 1:
            diag["y"].wait_recv()
            DB[z] = DS[...] + DR[...]
            diag[1] = (send(DB.at[z], DB.at[z], ZP), send(DB.at[z], DB.at[z], ZM))
        elif r <= 4:
            diag[r - 1][0].wait_recv()
            back = zi(1 - r)
            up = send(DB.at[back], DB.at[back], ZP)
            diag[r - 1][1].wait_recv()
            ahead = zi(r - 1)
            diag[r] = (up, send(DB.at[ahead], DB.at[ahead], ZM) if r < 4 else None)
        elif r == 5:
            diag[4][0].wait_recv()
            diag["y"].wait_send()
            DS[...] = jnp.sum(DB[...], axis=0) * (1.0 / COLS)

    stages = {0: gram, 1: stage1, 2: stage2, 3: lambda t: stage34(t, 1), 4: lambda t: stage34(t, 2), 5: stage5, 6: stage6}
    for r in range(START[-1] + 7):
        if 1 <= r <= 5:
            diag_step(r)
        for t in range(TICKS):
            if 1 <= r - START[t] <= 6:
                stages[r - START[t]](t)
        for t in range(TICKS):
            if r == START[t]:
                gram(t)
        if r == 14:
            pass_hop(0)
            pass_hop(2)
    moved[6].wait_recv()
    moved[7].wait_recv()

    sent_y, served, hops, hops_pair = {}, {}, {}, {}

    def unit(q):
        u = zi(q)
        return u, lax.div(u, 2), lax.rem(u, 2)

    def products(qs):
        n = len(qs)

        def body(t, _):
            lanes = pl.ds(pl.multiple_of(t * BLOCK, BLOCK), BLOCK)
            left = jnp.concatenate([G[zi(q), :, :, lanes].reshape(UNIT, BLOCK) for q in qs], axis=0)
            p = dot(left, N[t].reshape(BLOCK, WIDTH), 0)

            @pl.when(t == 0)
            def _():
                YA[0 : UNIT * n] = p

            @pl.when(t > 0)
            def _():
                YA[0 : UNIT * n] += p

            return 0

        lax.fori_loop(0, TICKS, body, 0)
        for i, q in enumerate(qs):
            u, half, odd = unit(q)
            Y[0, u] = YA[UNIT * i : UNIT * (i + 1)].astype(BF16)
            sent_y[q] = (
                send(Y.at[0, u], Y.at[2 + half, odd], XP),
                send(Y.at[0, u], Y.at[2 + half, 4 + odd], XM),
                send(Y.at[0, u], Y.at[1, u], CP),
            )
        for i, q in enumerate(qs):
            u = zi(q)
            rows = G[u].reshape(UNIT, ROWS).astype(F32)
            square = jnp.sum(rows * rows, axis=1, keepdims=True)
            here = lax.broadcasted_iota(jnp.int32, (UNIT, BLOCK), 0) + u * UNIT
            lanes = lax.broadcasted_iota(jnp.int32, (UNIT, BLOCK), 1)
            g = jnp.sum(jnp.where(here == lanes, DS[0:1], 0.0), axis=1, keepdims=True)
            half = g.astype(BF16).astype(F32)
            poly = (cubic_coef * g + quintic_coef * square).astype(BF16).astype(F32)
            fix = poly - (cubic_coef * half + quintic_coef * square)
            X[u] = linear_coef * X[u] + cubic_coef * YA[UNIT * i : UNIT * (i + 1)] + fix * N[0, u].astype(F32)

    def serve(qs):
        for q in qs:
            u, half, odd = unit(q)
            sent_y[q][0].wait_recv()
            if q in (0, 1, 2, 3):
                hops[q] = send(Y.at[2 + half, odd], Y.at[6, u], XP)
            a = send(Y.at[2 + half, odd], Y.at[2 + half, 2 + odd], CP)
            sent_y[q][1].wait_recv()
            if q not in (0, 1, 2, 3):
                hops[q] = send(Y.at[2 + half, 4 + odd], Y.at[6, u], XM)
            b = send(Y.at[2 + half, 4 + odd], Y.at[2 + half, 6 + odd], CP)
            served[q] = (a, b)

    def pass_y(qs):
        for q in qs:
            hops[q].wait_recv()
            u = zi(q)
            hops_pair[q] = send(Y.at[6, u], Y.at[7, u], CP)

    wide, thin = pl.ds(SPLIT, ROWS - SPLIT), pl.ds(0, SPLIT)
    to_y = {}
    to_y["thin"] = send(G.at[z, y, :, thin], G.at[z, y, :, thin], YP)
    own = [(send(G.at[z, y], G.at[z, y], ZP), send(G.at[z, y], G.at[z, y], ZM))]
    to_y[0] = [send(G.at[z, y, :, wide], G.at[z, y, :, wide], YP)]
    to_y["thin"].wait_recv()
    theirs = [
        (
            send(G.at[z, other, :, thin], G.at[z, other, :, thin], ZP),
            send(G.at[z, other, :, thin], G.at[z, other, :, thin], ZM),
        )
    ]
    pass_hop(1)
    pass_hop(3)
    to_y[0][0].wait_recv()
    for i in range(4):
        hop_pair[i].wait_recv()
    products([0])

    done = [[0]]
    for k in range(1, 5):
        qs = [-k, k] if k < 4 else [4]
        forward, to_y[k] = [], []
        for way, q, peer in ((0, -k, ZP), (1, k, ZM)):
            own[k - 1][way].wait_recv()
            u = zi(q)
            if k < 3:
                forward.append(send(G.at[u, y], G.at[u, y], peer))
            elif k == 3:
                part = pl.ds(ROWS // 2 * way, ROWS // 2)
                forward.append(send(G.at[u, y, :, part], G.at[u, y, :, part], peer))
            if k < 4:
                to_y[k].append(send(G.at[u, y, :, wide], G.at[u, y, :, wide], YP))
        if k == 4:
            u = zi(4)
            to_y[k].append(send(G.at[u, y, :, wide], G.at[u, y, :, wide], YP))
        own.append(forward)
        forward = []
        for way, q, peer in ((0, -k, ZP), (1, k, ZM)):
            theirs[k - 1][way].wait_recv()
            u = zi(q)
            if k < 3:
                forward.append(send(G.at[u, other, :, thin], G.at[u, other, :, thin], peer))
            elif k == 3:
                part = pl.ds(SPLIT // 2 * way, SPLIT // 2)
                forward.append(send(G.at[u, other, :, part], G.at[u, other, :, part], peer))
        theirs.append(forward)
        for copy in to_y[k]:
            copy.wait_recv()
        products(qs)
        serve(done[-1])
        if k >= 2:
            pass_y(done[-2])
        done.append(qs)

    def add_up(t, m):
        left = G[4 * m : 4 * m + 4, :, :, BLOCK * t : BLOCK * (t + 1)].reshape(256, BLOCK)
        p = dot(left, Y[t].reshape(BLOCK, WIDTH), 0)
        X[4 * m : 4 * m + 4] += quintic_coef * p.reshape(4, UNIT, WIDTH)

    for q in sent_y:
        sent_y[q][2].wait_recv()
    for t in (0, 1):
        for m in range(2):
            add_up(t, m)
    serve([4])
    pass_y([-3, 3])
    for q in served:
        served[q][0].wait_recv()
        served[q][1].wait_recv()
    for t in (2, 3, 4, 5):
        for m in range(2):
            add_up(t, m)
    pass_y([4])
    for m in range(2):
        add_up(6, m)
    for q in hops_pair:
        hops_pair[q].wait_recv()
    stores = []
    for m in range(2):
        add_up(7, m)
        for u in range(4 * m, 4 * m + 4):
            stores.append(pltpu.make_async_copy(X.at[u], o_ref.at[pl.ds(UNIT * u, UNIT)], lsem.at[u]))
            stores[-1].start()
    for copy in started:
        if copy is not diag["y"]:
            copy.wait_send()
    for store in stores:
        store.wait()


def shards(iterate):
    scratch = [
        pltpu.VMEM((8, UNIT, WIDTH), F32),
        pltpu.VMEM((TICKS, 8, UNIT, WIDTH), BF16),
        pltpu.VMEM((TICKS, 8, UNIT, WIDTH), BF16),
        pltpu.VMEM((TICKS, 8, 96, 256), F32),
        pltpu.VMEM((8, 2, 32, ROWS), BF16),
        pltpu.VMEM((TICKS, 2, 96, 128), BF16),
        pltpu.VMEM((TICKS, 2, 96, 128), BF16),
        pltpu.VMEM((TICKS, 2, 3, 96, 256), BF16),
        pltpu.VMEM((TICKS, 2, 3, 96, 256), BF16),
        pltpu.VMEM((TICKS, 8, 32, 256), BF16),
        pltpu.VMEM((TICKS, 8, 32, 256), BF16),
        pltpu.VMEM((TICKS, 32, 256), BF16),
        pltpu.VMEM((TICKS, 32, 256), BF16),
        pltpu.VMEM((2, 32, BLOCK), BF16),
        pltpu.VMEM((8, BLOCK), F32),
        pltpu.VMEM((8, BLOCK), F32),
        pltpu.VMEM((8, 8, BLOCK), F32),
        pltpu.VMEM((2 * UNIT, WIDTH), F32),
        pltpu.SemaphoreType.DMA((MESSAGES,)),
        pltpu.SemaphoreType.DMA((MESSAGES,)),
        pltpu.SemaphoreType.DMA((8,)),
    ]
    return pl.pallas_call(
        kernel,
        out_shape=jax.ShapeDtypeStruct(iterate.shape, F32),
        in_specs=[pl.BlockSpec(memory_space=pl.ANY)],
        out_specs=pl.BlockSpec(memory_space=pl.ANY),
        scratch_shapes=scratch,
        compiler_params=pltpu.CompilerParams(
            collective_id=0, has_side_effects=True, vmem_limit_bytes=60 * 1024 * 1024
        ),
        cost_estimate=pl.CostEstimate(flops=6 * BLOCK * ROWS * WIDTH, bytes_accessed=8 * BLOCK * WIDTH, transcendentals=0),
    )(iterate)


def solution(mesh):
    return jax.shard_map(
        shards,
        mesh=mesh,
        in_specs=(P(("mat", "band"), "col"),),
        out_specs=P(("mat", "band"), "col"),
        check_vma=False,
    )
```

time: 555 us -> 177 us (0.32)
  waiting for transfers between devices: 507 us -> 0 us
  Pallas kernels: 0 us -> 173 us
  matrix products: 27.8 us -> 0 us
  between operations: 13.1 us -> 0.01 us
    all_gather x4 -> x0, waiting for transfers between devices: 287 us -> none  [the longest x1 99.2 us: shards(): lax.all_gather(gram_tile.astype(jnp.bfloat16), 'col', axis=0, tiled=True)]
    reduce_scatter x1 -> x0, waiting for transfers between devices: 219 us -> none  [shards(): lax.psum_scatter(lax.dot_general(chosen, narrow, (((1,), (1,)), ((), ()))...]
    pallas_call x0 -> x1, Pallas kernels: none -> 173 us  [shards(): pl.pallas_call(kernel, out_shape=jax.ShapeDtypeStruct(iterate.shape, F32)...]
    dot_general x3 -> x0, matrix products: 27.8 us -> none  [the longest x1 11.8 us: shards(): lax.dot_general(chosen, narrow, (((1,), (1,)), ((), ())), preferred_eleme...]
  transfers between devices with their start and end apart: 5 -> 0, of which waited for: 5 -> 0; matrix products, arithmetic and copies ran while one was open for 0% -> 0% of each run, Pallas kernels for 0% -> 0%
where the time goes in v1:
time: 177 us
  Pallas kernels  173 us (98%)
  local copies, waits for them, and re-layouts  3.22 us (2%)
    pallas_call x1, Pallas kernels, shards(): pl.pallas_call(kernel, out_shape=jax.ShapeDtypeStruct(iterate.shape, F32)...  173 us

profile of v1, /device:TPU:1, one launch (start us, length us, event | category | flops | bytes accessed | tf_op | source)
XLA Modules:
  0.0 176.6 jit_solution(14096696366295940762)
XLA Ops:
  0.0 173.4 %shard_map.17 = f32[512,1152]{1,0:T(8,128)} custom-call(f32[512,1152]{1,0:T(8,128)} %x_ref.1), custom_call_target="tpu_custom_call" | custom-call | flops 14495514624 | bytes 4718592 | tf_op jit(solution)/shard_map/pallas_call | solution.py:405
  173.4 3.2 %copy.3 = f32[512,1152]{1,0:T(8,128)} copy(f32[512,1152]{1,0:T(8,128)} %shard_map.17) | data formatting | bytes 4718592

commit v2 on v1

v2 whole, which is shorter than its diff:
```python
import jax
import jax.numpy as jnp
from jax import lax
from jax.experimental import pallas as pl
from jax.experimental.pallas import tpu as pltpu
from jax.sharding import PartitionSpec as P

COLS = 18432
MESH = pl.DeviceIdType.MESH
linear_coef = 3.4445
cubic_coef = -4.775
quintic_coef = 2.0315

F32, BF16 = jnp.float32, jnp.bfloat16
BLOCK, WIDTH, TICKS, UNIT = 512, 1152, 8, 64
ROWS = BLOCK * TICKS
SPLIT = 1536
MESSAGES, SENDS = 216, 48
START = (0, 1, 2, 4, 5, 7, 7, 7)
FLIGHT = 4


def dot(a, b, contract):
    return lax.dot_general(a, b, (((1,), (contract,)), ((), ())), preferred_element_type=F32)


def kernel(x_ref, o_ref, X, N, Y, V, G, SA, RA, SH, RH, SB, RB, SC, RC, RD, YS, YR, FS, FR, GS, DS, DR, DB, YA, ssem, rsem, lsem):
    mat, band, col = lax.axis_index("mat"), lax.axis_index("band"), lax.axis_index("col")
    x, core = lax.div(band, 2), lax.rem(band, 2)
    z, y = lax.div(col, 2), lax.rem(col, 2)
    other = 1 - y

    def at_x(d):
        return (mat, lax.rem(x + d + 4, 4) * 2 + core, col)

    def zi(d):
        return lax.rem(z + d + 8, 8)

    def at_z(d):
        return (mat, band, zi(d) * 2 + y)

    XP, XM, ZP, ZM, ZPP, ZMM = at_x(1), at_x(-1), at_z(1), at_z(-1), at_z(2), at_z(-2)
    YP = (mat, band, z * 2 + other)
    ZPY, ZMY = (mat, band, zi(1) * 2 + other), (mat, band, zi(-1) * 2 + other)
    CP = (mat, x * 2 + 1 - core, col)

    started = []

    def send(src, dst, peer):
        n = len(started)
        if n >= SENDS:
            started[n - SENDS].wait_send()
        copy = pltpu.make_async_remote_copy(
            src_ref=src,
            dst_ref=dst,
            send_sem=ssem.at[n % SENDS],
            recv_sem=rsem.at[n],
            device_id=peer,
            device_id_type=MESH,
        )
        copy.start()
        started.append(copy)
        return copy

    loads = [pltpu.make_async_copy(x_ref.at[pl.ds(UNIT * u, UNIT)], X.at[u], lsem.at[u]) for u in range(8)]
    for load in loads:
        load.start()
    barrier = pltpu.get_barrier_semaphore()
    for peer in (XP, XM, ZP, ZM, ZPP, ZMM, ZPY, ZMY, YP, CP):
        pl.semaphore_signal(barrier, inc=1, device_id=peer, device_id_type=MESH)
    for u, load in enumerate(loads):
        load.wait()
        N[0, u] = X[u].astype(BF16)
    pl.semaphore_wait(barrier, 10)

    plus, minus, pair, hop, hop_pair = {}, {}, {}, {}, {}
    relay = {}

    def send_own(i):
        plus[i] = send(N.at[0, pl.ds(2 * i, 2)], N.at[2 + i, pl.ds(0, 2)], XP)
        minus[i] = send(N.at[0, pl.ds(2 * i, 2)], N.at[2 + i, pl.ds(4, 2)], XM)

    def send_hop(i):
        if i < 2:
            hop[i] = send(N.at[2 + i, pl.ds(0, 2)], N.at[6, pl.ds(2 * i, 2)], XP)
        else:
            hop[i] = send(N.at[2 + i, pl.ds(4, 2)], N.at[6, pl.ds(2 * i, 2)], XM)

    def pass_hop(i):
        hop[i].wait_recv()
        hop_pair[i] = send(N.at[6, pl.ds(2 * i, 2)], N.at[7, pl.ds(2 * i, 2)], CP)

    send_own(0)
    pair_block = send(N.at[0], N.at[1], CP)
    for i in range(1, FLIGHT):
        send_own(i)

    def arrive(t):
        if t == 1:
            pair_block.wait_recv()
        if 2 <= t <= 5:
            i = t - 2
            plus[i].wait_recv()
            relay[i, 0] = send(N.at[t, pl.ds(0, 2)], N.at[t, pl.ds(2, 2)], CP)
            minus[i].wait_recv()
            relay[i, 1] = send(N.at[t, pl.ds(4, 2)], N.at[t, pl.ds(6, 2)], CP)
            if i + FLIGHT < 4:
                send_own(i + FLIGHT)
            if i >= 2:
                send_hop(i - 2)
                send_hop(i)
            relay[i, 0].wait_recv()
            relay[i, 1].wait_recv()

    first, own_part, ring1, ring2, ring3, moved, diag = {}, {}, {}, {}, {}, {}, {}

    def height(t):
        return 96 if t < 6 else 128

    def gram(t):
        arrive(t)
        if t <= 5:
            right = N[t].reshape(BLOCK, WIDTH)
        elif t == 6:
            right = N[2:6, 4:6].reshape(BLOCK, WIDTH)
        else:
            right = N[2:6, 2:4].reshape(BLOCK, WIDTH)
        total = jnp.zeros((1, BLOCK), F32)
        for m in range(2):
            if t <= 5:
                left = N[0, 4 * m : 4 * m + 4].reshape(256, WIDTH)
            elif t == 6:
                left = N[2 + 2 * m : 4 + 2 * m, 0:2].reshape(256, WIDTH)
            else:
                left = N[2 + 2 * m : 4 + 2 * m, 4:6].reshape(256, WIDTH)
            p = dot(left, right, 1)
            if t == 0:
                rows = lax.broadcasted_iota(jnp.int32, (256, BLOCK), 0) + 256 * m
                lanes = lax.broadcasted_iota(jnp.int32, (256, BLOCK), 1)
                total += jnp.sum(jnp.where(rows == lanes, p, 0.0), axis=0, keepdims=True)
            p = p.reshape(4, UNIT, BLOCK)
            low, high = p[:, 0:32], p[:, 32:64]
            mine, rest = jnp.where(y == 0, low, high), jnp.where(y == 0, high, low)
            here = pl.ds(4 * m, 4)
            V[t, here, 0:32, :] = mine[:, :, 0:256]
            V[t, here, 32:64, :] = mine[:, :, 256:]
            V[t, here, 64:96, :] = rest[:, :, 0:256]
            if t < 6:
                YS[t, here] = rest[:, :, 256:].astype(BF16)
            else:
                V[t, here, 96:128, :] = rest[:, :, 256:]
        if t < 6:
            first[t] = send(YS.at[t], YR.at[t], YP)
        else:
            launch(t)
        if t == 0:
            DS[...] = jnp.broadcast_to(total, (8, BLOCK))
            diag["y"] = send(DS, DR, YP)

    def stage1(t):
        if t < 6:
            first[t].wait_recv()
            V[t, :, 32:64, :] += YR[t].astype(F32)
            launch(t)

    def launch(t):
        h = height(t)
        sent = []
        for way, peer, far in ((0, ZP, ZPP), (1, ZM, ZMM)):
            d = zi(3) if way == 0 else zi(-3)
            SA[t, way, 0:h] = V[t, d, 0:h].astype(BF16)
            sent.append(send(SA.at[t, way, pl.ds(0, h)], RA.at[t, way, pl.ds(0, h)], peer))
            SH[t, way, 0:h] = V[t, zi(4), 0:h, 128 * way : 128 * way + 128].astype(BF16)
            sent.append(send(SH.at[t, way, pl.ds(0, h)], RH.at[t, way, pl.ds(0, h)], far))
        ring1[t] = sent
        FS[t, 0 : h - 64] = V[t, z, 64:h].astype(BF16)
        own_part[t] = send(FS.at[t, pl.ds(0, h - 64)], FR.at[t, pl.ds(0, h - 64)], YP)

    def stage2(t):
        h = height(t)
        sent = []
        for way, peer in ((0, ZP), (1, ZM)):
            ring1[t][2 * way].wait_recv()
            ring1[t][2 * way + 1].wait_recv()
            d = zi(2) if way == 0 else zi(-2)
            half, rest = pl.ds(128 * way, 128), pl.ds(128 - 128 * way, 128)
            SB[t, way, 0:h, half] = (
                V[t, d, 0:h, half] + RA[t, way, 0:h, half].astype(F32) + RH[t, way, 0:h].astype(F32)
            ).astype(BF16)
            SB[t, way, 0:h, rest] = (V[t, d, 0:h, rest] + RA[t, way, 0:h, rest].astype(F32)).astype(BF16)
            sent.append(send(SB.at[t, way, pl.ds(0, h)], RB.at[t, way, pl.ds(0, h)], peer))
        ring2[t] = sent

    def stage3(t):
        h = height(t)
        sent = []
        for way, peer, across in ((0, ZP, ZPY), (1, ZM, ZMY)):
            ring2[t][way].wait_recv()
            d = zi(1) if way == 0 else zi(-1)
            SC[t, way, 0:h] = (V[t, d, 0:h] + RB[t, way, 0:h].astype(F32)).astype(BF16)
            sent.append(send(SC.at[t, way, pl.ds(0, 64)], RC.at[t, way], peer))
            sent.append(send(SC.at[t, way, pl.ds(64, h - 64)], RD.at[t, way, pl.ds(0, h - 64)], across))
        ring3[t] = sent

    def stage4(t):
        for copy in ring3[t]:
            copy.wait_recv()
        own_part[t].wait_recv()
        r = V[t, z, 0:64] + RC[t, 0].astype(F32) + RC[t, 1].astype(F32)
        n = height(t) - 64
        cross = RD[t, 0, 0:n].astype(F32) + RD[t, 1, 0:n].astype(F32) + FR[t, 0:n].astype(F32)
        low, high = r[0:32] + cross[0:32], r[32:64]
        if n == 64:
            high = high + cross[32:64]
        g = (jnp.concatenate([low, high], axis=1) * (1.0 / COLS)).astype(BF16)
        if t < 6:
            G[z, y, :, BLOCK * t : BLOCK * (t + 1)] = g
        else:
            GS[t - 6] = g
            there = G.at[z, y, :, pl.ds(BLOCK * t, BLOCK)]
            moved[t] = send(GS.at[t - 6], there, XM if t == 6 else XP)

    def stage5(t):
        if t >= 6:
            moved[t].wait_recv()

    def diag_step(r):
        if r == 1:
            diag["y"].wait_recv()
            DB[z] = DS[...] + DR[...]
            diag[1] = (send(DB.at[z], DB.at[z], ZP), send(DB.at[z], DB.at[z], ZM))
        elif r <= 4:
            diag[r - 1][0].wait_recv()
            back = zi(1 - r)
            up = send(DB.at[back], DB.at[back], ZP)
            diag[r - 1][1].wait_recv()
            ahead = zi(r - 1)
            diag[r] = (up, send(DB.at[ahead], DB.at[ahead], ZM) if r < 4 else None)
        elif r == 5:
            diag[4][0].wait_recv()
            DR[...] = jnp.sum(DB[...], axis=0) * (1.0 / COLS)
        elif r == 6:
            rows = lax.broadcasted_iota(jnp.int32, (32, BLOCK), 0) + (z * 64 + y * 32)
            lanes = lax.broadcasted_iota(jnp.int32, (32, BLOCK), 1)
            G[z, y, :, 0:BLOCK] = jnp.where(rows == lanes, DR[0:1].astype(BF16), G[z, y, :, 0:BLOCK])

    plan = [gram, stage1, stage2, stage3, stage4, stage5]
    for r in range(START[-1] + 5):
        if r >= 1:
            diag_step(r)
        for t in range(TICKS):
            n = r - START[t] + (1 if t >= 6 and r > START[t] else 0)
            if 1 <= n <= 5:
                plan[n](t)
        for t in range(TICKS):
            if r == START[t]:
                gram(t)
        if r == 9:
            pass_hop(0)
            pass_hop(2)

    sent_y, served, hops, hops_pair = {}, {}, {}, {}

    def unit(q):
        u = zi(q)
        return u, lax.div(u, 2), lax.rem(u, 2)

    def products(qs):
        n = len(qs)

        def body(t, _):
            lanes = pl.ds(pl.multiple_of(t * BLOCK, BLOCK), BLOCK)
            left = jnp.concatenate([G[zi(q), :, :, lanes].reshape(UNIT, BLOCK) for q in qs], axis=0)
            p = dot(left, N[t].reshape(BLOCK, WIDTH), 0)

            @pl.when(t == 0)
            def _():
                YA[0 : UNIT * n] = p

            @pl.when(t > 0)
            def _():
                YA[0 : UNIT * n] += p

            return 0

        lax.fori_loop(0, TICKS, body, 0)
        for i, q in enumerate(qs):
            u, half, odd = unit(q)
            Y[0, u] = YA[UNIT * i : UNIT * (i + 1)].astype(BF16)
            sent_y[q] = (
                send(Y.at[0, u], Y.at[2 + half, odd], XP),
                send(Y.at[0, u], Y.at[2 + half, 4 + odd], XM),
                send(Y.at[0, u], Y.at[1, u], CP),
            )
        for i, q in enumerate(qs):
            u = zi(q)
            rows = G[u].reshape(UNIT, ROWS).astype(F32)
            square = jnp.sum(rows * rows, axis=1, keepdims=True)
            here = lax.broadcasted_iota(jnp.int32, (UNIT, BLOCK), 0) + u * UNIT
            lanes = lax.broadcasted_iota(jnp.int32, (UNIT, BLOCK), 1)
            g = jnp.sum(jnp.where(here == lanes, DR[0:1], 0.0), axis=1, keepdims=True)
            half = g.astype(BF16).astype(F32)
            poly = (cubic_coef * g + quintic_coef * square).astype(BF16).astype(F32)
            fix = poly - (cubic_coef * half + quintic_coef * square)
            X[u] = linear_coef * X[u] + cubic_coef * YA[UNIT * i : UNIT * (i + 1)] + fix * N[0, u].astype(F32)

    def serve(qs):
        for q in qs:
            u, half, odd = unit(q)
            sent_y[q][0].wait_recv()
            if q in (0, 1, 2, 3):
                hops[q] = send(Y.at[2 + half, odd], Y.at[6, u], XP)
            a = send(Y.at[2 + half, odd], Y.at[2 + half, 2 + odd], CP)
            sent_y[q][1].wait_recv()
            if q not in (0, 1, 2, 3):
                hops[q] = send(Y.at[2 + half, 4 + odd], Y.at[6, u], XM)
            b = send(Y.at[2 + half, 4 + odd], Y.at[2 + half, 6 + odd], CP)
            served[q] = (a, b)

    def pass_y(qs):
        for q in qs:
            hops[q].wait_recv()
            u = zi(q)
            hops_pair[q] = send(Y.at[6, u], Y.at[7, u], CP)

    wide, thin = pl.ds(SPLIT, ROWS - SPLIT), pl.ds(0, SPLIT)
    half_own = (pl.ds(0, ROWS // 2), pl.ds(ROWS // 2, ROWS // 2))
    half_thin = (pl.ds(0, SPLIT // 2), pl.ds(SPLIT // 2, SPLIT // 2))
    own, theirs, to_y = {}, {}, {}

    def rows_to(q, rows, part, peer):
        ref = G.at[zi(q), rows, :, part]
        return send(ref, ref, peer)

    def take_own(k):
        for part in (0, 1):
            for way, q, peer in ((0, -k, ZP), (1, k, ZM)):
                if k < 4 or part == way:
                    own[k, part, way].wait_recv()
                if k < 3 or (k == 3 and part == way):
                    own[k + 1, part, way] = rows_to(q, y, half_own[part], peer)
        for q in (-k, k) if k < 4 else (4,):
            to_y[q] = rows_to(q, y, wide, YP)

    def take_theirs(k):
        for way, q, peer in ((0, -k, ZP), (1, k, ZM)):
            theirs[k, way].wait_recv()
            if k < 3:
                theirs[k + 1, way] = rows_to(q, other, thin, peer)
            elif k == 3:
                theirs[k + 1, way] = rows_to(q, other, half_thin[way], peer)

    thin_y = rows_to(0, y, thin, YP)
    for part in (0, 1):
        for way, peer in ((0, ZP), (1, ZM)):
            own[1, part, way] = rows_to(0, y, half_own[part], peer)
    to_y[0] = rows_to(0, y, wide, YP)
    thin_y.wait_recv()
    for way, peer in ((0, ZP), (1, ZM)):
        theirs[1, way] = rows_to(0, other, thin, peer)
    pass_hop(1)
    pass_hop(3)
    take_own(1)
    for i in range(4):
        hop_pair[i].wait_recv()

    done = []
    for k in range(5):
        qs = [0] if k == 0 else [-k, k] if k < 4 else [4]
        if 1 <= k < 4:
            take_own(k + 1)
        for q in qs:
            to_y[q].wait_recv()
        products(qs)
        if k < 4:
            take_theirs(k + 1)
        if k >= 1:
            serve(done[-1])
        if k >= 2:
            pass_y(done[-2])
        done.append(qs)

    def add_up(t, m):
        left = G[4 * m : 4 * m + 4, :, :, BLOCK * t : BLOCK * (t + 1)].reshape(256, BLOCK)
        p = dot(left, Y[t].reshape(BLOCK, WIDTH), 0)
        X[4 * m : 4 * m + 4] += quintic_coef * p.reshape(4, UNIT, WIDTH)

    for q in sent_y:
        sent_y[q][2].wait_recv()
    for t in (0, 1):
        for m in range(2):
            add_up(t, m)
    serve([4])
    pass_y([-3, 3])
    for q in served:
        served[q][0].wait_recv()
        served[q][1].wait_recv()
    for t in (2, 3, 4, 5):
        for m in range(2):
            add_up(t, m)
    pass_y([4])
    for m in range(2):
        add_up(6, m)
    for q in hops_pair:
        hops_pair[q].wait_recv()
    stores = []
    for m in range(2):
        add_up(7, m)
        for u in range(4 * m, 4 * m + 4):
            stores.append(pltpu.make_async_copy(X.at[u], o_ref.at[pl.ds(UNIT * u, UNIT)], lsem.at[u]))
            stores[-1].start()
    for copy in started[-SENDS:]:
        copy.wait_send()
    for store in stores:
        store.wait()


def shards(iterate):
    scratch = [
        pltpu.VMEM((8, UNIT, WIDTH), F32),
        pltpu.VMEM((TICKS, 8, UNIT, WIDTH), BF16),
        pltpu.VMEM((TICKS, 8, UNIT, WIDTH), BF16),
        pltpu.VMEM((TICKS, 8, 128, 256), F32),
        pltpu.VMEM((8, 2, 32, ROWS), BF16),
        pltpu.VMEM((TICKS, 2, 128, 256), BF16),
        pltpu.VMEM((TICKS, 2, 128, 256), BF16),
        pltpu.VMEM((TICKS, 2, 128, 128), BF16),
        pltpu.VMEM((TICKS, 2, 128, 128), BF16),
        pltpu.VMEM((TICKS, 2, 128, 256), BF16),
        pltpu.VMEM((TICKS, 2, 128, 256), BF16),
        pltpu.VMEM((TICKS, 2, 128, 256), BF16),
        pltpu.VMEM((TICKS, 2, 64, 256), BF16),
        pltpu.VMEM((TICKS, 2, 64, 256), BF16),
        pltpu.VMEM((6, 8, 32, 256), BF16),
        pltpu.VMEM((6, 8, 32, 256), BF16),
        pltpu.VMEM((TICKS, 64, 256), BF16),
        pltpu.VMEM((TICKS, 64, 256), BF16),
        pltpu.VMEM((2, 32, BLOCK), BF16),
        pltpu.VMEM((8, BLOCK), F32),
        pltpu.VMEM((8, BLOCK), F32),
        pltpu.VMEM((8, 8, BLOCK), F32),
        pltpu.VMEM((2 * UNIT, WIDTH), F32),
        pltpu.SemaphoreType.DMA((MESSAGES,)),
        pltpu.SemaphoreType.DMA((MESSAGES,)),
        pltpu.SemaphoreType.DMA((8,)),
    ]
    return pl.pallas_call(
        kernel,
        out_shape=jax.ShapeDtypeStruct(iterate.shape, F32),
        in_specs=[pl.BlockSpec(memory_space=pl.ANY)],
        out_specs=pl.BlockSpec(memory_space=pl.ANY),
        scratch_shapes=scratch,
        compiler_params=pltpu.CompilerParams(
            collective_id=0, has_side_effects=True, vmem_limit_bytes=60 * 1024 * 1024
        ),
        cost_estimate=pl.CostEstimate(flops=6 * BLOCK * ROWS * WIDTH, bytes_accessed=8 * BLOCK * WIDTH, transcendentals=0),
    )(iterate)


def solution(mesh):
    return jax.shard_map(
        shards,
        mesh=mesh,
        in_specs=(P(("mat", "band"), "col"),),
        out_specs=P(("mat", "band"), "col"),
        check_vma=False,
    )
```

time: 177 us -> 148 us (0.84)
  Pallas kernels: 173 us -> 145 us
    pallas_call x1, Pallas kernels: 173 us -> 145 us  [shards(): pl.pallas_call(kernel, out_shape=jax.ShapeDtypeStruct(iterate.shape, F32)...]
where the time goes in v2:
time: 148 us
  Pallas kernels  145 us (98%)
  local copies, waits for them, and re-layouts  3.22 us (2%)
    pallas_call x1, Pallas kernels, shards(): pl.pallas_call(kernel, out_shape=jax.ShapeDtypeStruct(iterate.shape, F32)...  145 us
    unnamed x1, local copies, waits for them, and re-layouts  3.22 us

profile of v2, /device:TPU:1, one launch (start us, length us, event | category | flops | bytes accessed | tf_op | source)
XLA Modules:
  0.0 148.1 jit_solution(8442652054113886754)
XLA Ops:
  0.0 144.9 %shard_map.17 = f32[512,1152]{1,0:T(8,128)} custom-call(f32[512,1152]{1,0:T(8,128)} %x_ref.1), custom_call_target="tpu_custom_call" | custom-call | flops 14495514624 | bytes 4718592 | tf_op jit(solution)/shard_map/pallas_call | solution.py:447
  144.9 3.2 %copy.3 = f32[512,1152]{1,0:T(8,128)} copy(f32[512,1152]{1,0:T(8,128)} %shard_map.17) | data formatting | bytes 4718592

commit v3 on v2

--- a/solution.py
+++ b/solution.py
@@ -15,8 +15,8 @@
 BLOCK, WIDTH, TICKS, UNIT = 512, 1152, 8, 64
 ROWS = BLOCK * TICKS
 SPLIT = 1536
-MESSAGES, SENDS = 216, 48
-START = (0, 1, 2, 4, 5, 7, 7, 7)
+MESSAGES, SENDS = 222, 48
+START = (0, 1, 2, 3, 4, 5, 5, 5)
 FLIGHT = 4
 
 
@@ -202,6 +202,12 @@
             sent.append(send(SC.at[t, way, pl.ds(64, h - 64)], RD.at[t, way, pl.ds(0, h - 64)], across))
         ring3[t] = sent
 
+    early = {}
+
+    def tell(t):
+        ref = G.at[z, y, :, pl.ds(BLOCK * t, BLOCK)]
+        early[t] = send(ref, ref, YP)
+
     def stage4(t):
         for copy in ring3[t]:
             copy.wait_recv()
@@ -215,6 +221,8 @@
         g = (jnp.concatenate([low, high], axis=1) * (1.0 / COLS)).astype(BF16)
         if t < 6:
             G[z, y, :, BLOCK * t : BLOCK * (t + 1)] = g
+            if t > 0:
+                tell(t)
         else:
             GS[t - 6] = g
             there = G.at[z, y, :, pl.ds(BLOCK * t, BLOCK)]
@@ -223,6 +231,7 @@
     def stage5(t):
         if t >= 6:
             moved[t].wait_recv()
+            tell(t)
 
     def diag_step(r):
         if r == 1:
@@ -243,6 +252,16 @@
             rows = lax.broadcasted_iota(jnp.int32, (32, BLOCK), 0) + (z * 64 + y * 32)
             lanes = lax.broadcasted_iota(jnp.int32, (32, BLOCK), 1)
             G[z, y, :, 0:BLOCK] = jnp.where(rows == lanes, DR[0:1].astype(BF16), G[z, y, :, 0:BLOCK])
+            tell(0)
+
+    wide, thin = pl.ds(SPLIT, ROWS - SPLIT), pl.ds(0, SPLIT)
+    half_own = (pl.ds(0, ROWS // 2), pl.ds(ROWS // 2, ROWS // 2))
+    half_thin = (pl.ds(0, SPLIT // 2), pl.ds(SPLIT // 2, SPLIT // 2))
+    own, theirs, to_y = {}, {}, {}
+
+    def rows_to(q, rows, part, peer):
+        ref = G.at[zi(q), rows, :, part]
+        return send(ref, ref, peer)
 
     plan = [gram, stage1, stage2, stage3, stage4, stage5]
     for r in range(START[-1] + 5):
@@ -255,9 +274,13 @@
         for t in range(TICKS):
             if r == START[t]:
                 gram(t)
-        if r == 9:
-            pass_hop(0)
-            pass_hop(2)
+        if r == START[-1] + 3:
+            for way, peer in ((0, ZP), (1, ZM)):
+                own[1, 0, way] = rows_to(0, y, half_own[0], peer)
+            for t in (0, 1, 2):
+                early[t].wait_recv()
+            for way, peer in ((0, ZP), (1, ZM)):
+                theirs[1, way] = rows_to(0, other, thin, peer)
 
     sent_y, served, hops, hops_pair = {}, {}, {}, {}
 
@@ -323,15 +346,6 @@
             u = zi(q)
             hops_pair[q] = send(Y.at[6, u], Y.at[7, u], CP)
 
-    wide, thin = pl.ds(SPLIT, ROWS - SPLIT), pl.ds(0, SPLIT)
-    half_own = (pl.ds(0, ROWS // 2), pl.ds(ROWS // 2, ROWS // 2))
-    half_thin = (pl.ds(0, SPLIT // 2), pl.ds(SPLIT // 2, SPLIT // 2))
-    own, theirs, to_y = {}, {}, {}
-
-    def rows_to(q, rows, part, peer):
-        ref = G.at[zi(q), rows, :, part]
-        return send(ref, ref, peer)
-
     def take_own(k):
         for part in (0, 1):
             for way, q, peer in ((0, -k, ZP), (1, k, ZM)):
@@ -350,32 +364,28 @@
             elif k == 3:
                 theirs[k + 1, way] = rows_to(q, other, half_thin[way], peer)
 
-    thin_y = rows_to(0, y, thin, YP)
-    for part in (0, 1):
-        for way, peer in ((0, ZP), (1, ZM)):
-            own[1, part, way] = rows_to(0, y, half_own[part], peer)
-    to_y[0] = rows_to(0, y, wide, YP)
-    thin_y.wait_recv()
     for way, peer in ((0, ZP), (1, ZM)):
-        theirs[1, way] = rows_to(0, other, thin, peer)
-    pass_hop(1)
-    pass_hop(3)
-    take_own(1)
+        own[1, 1, way] = rows_to(0, y, half_own[1], peer)
+    for i in (0, 2, 1, 3):
+        pass_hop(i)
+    for t in range(3, TICKS):
+        early[t].wait_recv()
     for i in range(4):
         hop_pair[i].wait_recv()
 
     done = []
     for k in range(5):
         qs = [0] if k == 0 else [-k, k] if k < 4 else [4]
-        if 1 <= k < 4:
+        if k < 4:
             take_own(k + 1)
-        for q in qs:
-            to_y[q].wait_recv()
+        if k >= 1:
+            for q in qs:
+                to_y[q].wait_recv()
         products(qs)
+        if k >= 1:
+            serve(done[-1])
         if k < 4:
             take_theirs(k + 1)
-        if k >= 1:
-            serve(done[-1])
         if k >= 2:
             pass_y(done[-2])
         done.append(qs)

time: 148 us -> 138 us (0.932)
  Pallas kernels: 145 us -> 134 us
    pallas_call x1, Pallas kernels: 145 us -> 134 us  [shards(): pl.pallas_call(kernel, out_shape=jax.ShapeDtypeStruct(iterate.shape, F32)...]
where the time goes in v3:
time: 138 us
  Pallas kernels  134 us (97%)
  local copies, waits for them, and re-layouts  3.22 us (2%)
    pallas_call x1, Pallas kernels, shards(): pl.pallas_call(kernel, out_shape=jax.ShapeDtypeStruct(iterate.shape, F32)...  134 us
    unnamed x1, local copies, waits for them, and re-layouts  3.22 us

profile of v3, /device:TPU:1, one launch (start us, length us, event | category | flops | bytes accessed | tf_op | source)
XLA Modules:
  0.0 137.6 jit_solution(1656204169208507188)
XLA Ops:
  0.0 134.4 %shard_map.17 = f32[512,1152]{1,0:T(8,128)} custom-call(f32[512,1152]{1,0:T(8,128)} %x_ref.1), custom_call_target="tpu_custom_call" | custom-call | flops 14495514624 | bytes 4718592 | tf_op jit(solution)/shard_map/pallas_call | solution.py:457
  134.4 3.2 %copy.3 = f32[512,1152]{1,0:T(8,128)} copy(f32[512,1152]{1,0:T(8,128)} %shard_map.17) | data formatting | bytes 4718592

commit v4 on v3

--- a/solution.py
+++ b/solution.py
@@ -265,14 +265,17 @@
 
     plan = [gram, stage1, stage2, stage3, stage4, stage5]
     for r in range(START[-1] + 5):
+        for t in range(TICKS) if r == START[-1] else ():
+            if r == START[t]:
+                gram(t)
         if r >= 1:
             diag_step(r)
-        for t in range(TICKS):
+        for t in reversed(range(TICKS)) if r > START[-1] else range(TICKS):
             n = r - START[t] + (1 if t >= 6 and r > START[t] else 0)
             if 1 <= n <= 5:
                 plan[n](t)
         for t in range(TICKS):
-            if r == START[t]:
+            if r == START[t] and r < START[-1]:
                 gram(t)
         if r == START[-1] + 3:
             for way, peer in ((0, ZP), (1, ZM)):

time: 138 us -> 136 us (0.986)
  Pallas kernels: 134 us -> 132 us
    pallas_call x1, Pallas kernels: 134 us -> 132 us  [shards(): pl.pallas_call(kernel, out_shape=jax.ShapeDtypeStruct(iterate.shape, F32)...]
where the time goes in v4:
time: 136 us; the launch traced here: 135 us
  Pallas kernels  132 us (97%)
  local copies, waits for them, and re-layouts  3.22 us (2%)
    pallas_call x1, Pallas kernels, shards(): pl.pallas_call(kernel, out_shape=jax.ShapeDtypeStruct(iterate.shape, F32)...  132 us
    unnamed x1, local copies, waits for them, and re-layouts  3.22 us

profile of v4, /device:TPU:1, one launch (start us, length us, event | category | flops | bytes accessed | tf_op | source)
XLA Modules:
  0.0 135.5 jit_solution(4450497086116446863)
XLA Ops:
  0.0 132.2 %shard_map.17 = f32[512,1152]{1,0:T(8,128)} custom-call(f32[512,1152]{1,0:T(8,128)} %x_ref.1), custom_call_target="tpu_custom_call" | custom-call | flops 14495514624 | bytes 4718592 | tf_op jit(solution)/shard_map/pallas_call | solution.py:460
  132.3 3.2 %copy.3 = f32[512,1152]{1,0:T(8,128)} copy(f32[512,1152]{1,0:T(8,128)} %shard_map.17) | data formatting | bytes 4718592
